TPU v7x, 32 devices: a whole 2x2x4 slice. The times are simulated.
32 devices in a mesh: ma: 2 (over y), an: 16 (over z, x, core).
Axes of the slice: x: 2, y: 2, z: 4, core: 2. Of those that a mesh axis runs over, the one named last changes fastest.
Arguments:
- tokens: bfloat16 [64, 512, 768], P(('ma', 'an')), may hold values from -6 to 6
- tasks: int32 [64], P(('ma', 'an')), may hold values from 0 to 7
- segments: int32 [64, 512], P(('ma', 'an')), may hold values from 0 to 3, never falling along the last dimension, each value on 1 to 256 neighbouring positions
- buckets: int32 [1023], replicated, may hold values from 0 to 31
- w_query: bfloat16 [768, 768], replicated, may hold values from -0.21875 to 0.21875
- w_key: bfloat16 [768, 768], replicated, may hold values from -0.21875 to 0.21875
- w_value: bfloat16 [768, 768], replicated, may hold values from -0.21875 to 0.21875
- w_out: bfloat16 [768, 768], replicated, may hold values from -1.75 to 1.75
- w_up: bfloat16 [768, 3072], P('ma', 'an'), may hold values from -0.21875 to 0.21875
- w_down: bfloat16 [3072, 768], P('an', 'ma'), may hold values from -0.109375 to 0.109375
- bias_table: float32 [8, 32, 12], replicated, may hold values from -6 to 6
- gain_attn: float32 [768], replicated, may hold values from 0.5 to 1.5
- gain_ffn: float32 [768], replicated, may hold values from 0.5 to 1.5
- cotangent: bfloat16 [64, 512, 768], P(('ma', 'an')), may hold values from -6 to 6
Outputs:
- output: bfloat16 [64, 512, 768], P(('ma', 'an'))
- grad_tokens: float32 [64, 512, 768], P(('ma', 'an'))
- grad_query: float32 [768, 768], replicated
- grad_key: float32 [768, 768], replicated
- grad_value: float32 [768, 768], replicated
- grad_w_out: float32 [768, 768], replicated
- grad_up: float32 [768, 3072], P('ma', 'an')
- grad_down: float32 [3072, 768], P('an', 'ma')
- grad_table: float32 [8, 32, 12], replicated
- grad_gain_attn: float32 [768], replicated
- grad_gain_ffn: float32 [768], replicated
Inputs may be any that keep to these rules, and one draw needn't show every extreme that they name: `segments`: within a row segment numbers never fall; a token attends only to tokens of its own segment.
All inputs are finite; a program needn't handle non-finite values.
Results may differ from a plain program's by a relative error of at most 0.015.
Values may be sent and summed in bfloat16 or wider, within the bound.
No kernel may reach another device: no remote copies, remote signals or barrier semaphores. Data moves between devices by JAX's collectives and lax.ppermute only.
A program may use at most 256 MiB of HBM per device.

v0:
```python
import jax
import jax.numpy as jnp
from jax import lax
from jax.sharding import PartitionSpec as P

epsilon = 1e-06
highest = lax.Precision.HIGHEST


def rms_scale(values, gain_vec):
    return (
        values * lax.rsqrt(jnp.mean(values * values, axis=-1, keepdims=True) + epsilon) * gain_vec
    )


def smooth_gate(values):
    return jax.nn.gelu(values, approximate=True)


def spread_offsets(per_offset, length):
    heads = per_offset.shape[0]
    padded = jnp.pad(per_offset, ((0, 0), (0, 1)))
    tiled = jnp.tile(padded, (1, length))[:, : length * (2 * length - 1)]
    return tiled.reshape(heads, length, 2 * length - 1)[:, :, length - 1 :]


def diagonal_sums(grid, length):
    heads = grid.shape[0]
    wide = jnp.pad(grid, ((0, 0), (0, 0), (length - 1, 0)))
    flat = jnp.pad(wide.reshape(heads, length * (2 * length - 1)), ((0, 0), (0, length)))
    return jnp.sum(flat.reshape(heads, length, 2 * length), axis=1)[:, : 2 * length - 1]


def local(
    tokens,
    tasks,
    segments,
    buckets,
    w_query,
    w_key,
    w_value,
    w_out,
    w_up,
    w_down,
    bias_table,
    gain_attn,
    gain_ffn,
    cotangent,
):
    row_count = tokens.shape[0]
    length = tokens.shape[1]
    width = tokens.shape[2]
    groups = bias_table.shape[0]
    bucket_count = bias_table.shape[1]
    heads = bias_table.shape[2]
    head_dim = width // heads
    scale = float(head_dim) ** (-0.5)
    total = row_count * length
    flat_tokens = tokens.astype(jnp.float32).reshape(total, width)
    part_up, part_down = (
        lax.all_gather(w_up, "ma", axis=0, tiled=True),
        lax.all_gather(w_down, "ma", axis=1, tiled=True),
    )
    up_full, down_full = (
        lax.all_gather(part_up, "an", axis=1, tiled=True),
        lax.all_gather(part_down, "an", axis=0, tiled=True),
    )
    normed_f, norm_pull = jax.vjp(rms_scale, flat_tokens, gain_attn)
    normed = normed_f.astype(jnp.bfloat16)
    joined_w = jnp.concatenate((w_query, w_key, w_value), axis=1)
    projected = jnp.dot(normed, joined_w, preferred_element_type=jnp.float32).astype(jnp.bfloat16)
    shape_heads = (row_count, length, heads, head_dim)
    queries = projected[:, :width].reshape(shape_heads)
    key_rows = projected[:, width : 2 * width].reshape(shape_heads)
    value_rows = projected[:, 2 * width :].reshape(shape_heads)
    bucket_hot = (buckets[None, :] == jnp.arange(bucket_count, dtype=jnp.int32)[:, None]).astype(
        jnp.float32
    )
    task_onehot = (tasks[:, None] == jnp.arange(groups, dtype=jnp.int32)[None, :]).astype(
        jnp.float32
    )
    table_rows = jnp.einsum("rg,gbh->rbh", task_onehot, bias_table, precision=highest)
    offset_bias = jnp.einsum("rbh,bk->rhk", table_rows, bucket_hot, precision=highest)

    def row_scores(row_queries, row_keys, row_offsets, seg_ids):
        bias_map = spread_offsets(row_offsets, length)
        scores = (
            jnp.einsum("ihd,jhd->hij", row_queries, row_keys, preferred_element_type=jnp.float32)
            * scale
            + bias_map
        )
        matching = seg_ids[:, None] == seg_ids[None, :]
        return jnp.where(matching[None], scores, -1e30)

    def row_forward(pieces):
        row_queries, row_keys, row_values, row_offsets, seg_ids = pieces
        scores = row_scores(row_queries, row_keys, row_offsets, seg_ids)
        peak = jnp.max(scores, axis=-1, keepdims=True)
        log_total = peak + jnp.log(jnp.sum(jnp.exp(scores - peak), axis=-1, keepdims=True))
        probs_low = jnp.exp(scores - log_total).astype(jnp.bfloat16)
        mixed_row = jnp.einsum(
            "hij,jhd->ihd", probs_low, row_values, preferred_element_type=jnp.float32
        )
        return (mixed_row.astype(jnp.bfloat16), log_total)

    mixed_heads, log_totals = lax.map(
        row_forward, (queries, key_rows, value_rows, offset_bias, segments)
    )
    mixed_flat = mixed_heads.reshape(total, width)
    middle = flat_tokens + jnp.dot(mixed_flat, w_out, preferred_element_type=jnp.float32)
    second_f, second_pull = jax.vjp(rms_scale, middle, gain_ffn)
    second = second_f.astype(jnp.bfloat16)
    up_proj = jnp.dot(second, up_full, preferred_element_type=jnp.float32)
    hidden_f, gate_pull = jax.vjp(smooth_gate, up_proj)
    hidden = hidden_f.astype(jnp.bfloat16)
    ffn_out = jnp.dot(hidden, down_full, preferred_element_type=jnp.float32)
    output = (middle + ffn_out).astype(jnp.bfloat16).reshape(row_count, length, width)
    upstream = cotangent.astype(jnp.float32).reshape(total, width)
    upstream_low = cotangent.reshape(total, width)
    grad_down_full = jnp.einsum(
        "nf,nd->fd", hidden, upstream_low, preferred_element_type=jnp.float32
    )
    grad_hidden = jnp.einsum(
        "nd,fd->nf", upstream_low, down_full, preferred_element_type=jnp.float32
    )
    grad_up_pre = gate_pull(grad_hidden)[0].astype(jnp.bfloat16)
    grad_up_full = jnp.einsum("nd,nf->df", second, grad_up_pre, preferred_element_type=jnp.float32)
    grad_second = jnp.einsum("nf,df->nd", grad_up_pre, up_full, preferred_element_type=jnp.float32)
    grad_mid_part, grad_gain_ffn = second_pull(grad_second)
    grad_middle = upstream + grad_mid_part
    grad_attn_low = grad_middle.astype(jnp.bfloat16)
    grad_w_out = jnp.einsum(
        "nd,ne->de", mixed_flat, grad_attn_low, preferred_element_type=jnp.float32
    )
    grad_mixed = jnp.einsum("ne,de->nd", grad_attn_low, w_out, preferred_element_type=jnp.float32)
    grad_mixed = grad_mixed.astype(jnp.bfloat16).reshape(shape_heads)

    def row_backward(pieces):
        row_queries, row_keys, row_values, row_offsets, seg_ids, log_total, grad_row = pieces
        scores = row_scores(row_queries, row_keys, row_offsets, seg_ids)
        probs = jnp.exp(scores - log_total)
        probs_low = probs.astype(jnp.bfloat16)
        grad_values = jnp.einsum(
            "hij,ihd->jhd", probs_low, grad_row, preferred_element_type=jnp.float32
        ).astype(jnp.bfloat16)
        grad_probs = jnp.einsum(
            "ihd,jhd->hij", grad_row, row_values, preferred_element_type=jnp.float32
        )
        centre = jnp.sum(probs * grad_probs, axis=-1, keepdims=True)
        grad_scores = (probs * (grad_probs - centre)).astype(jnp.bfloat16)
        grad_queries = (
            jnp.einsum("hij,jhd->ihd", grad_scores, row_keys, preferred_element_type=jnp.float32)
            * scale
        ).astype(jnp.bfloat16)
        grad_keys = (
            jnp.einsum("hij,ihd->jhd", grad_scores, row_queries, preferred_element_type=jnp.float32)
            * scale
        ).astype(jnp.bfloat16)
        grad_offsets = diagonal_sums(grad_scores.astype(jnp.float32), length)
        return (grad_queries, grad_keys, grad_values, grad_offsets)

    grad_queries, grad_keys, grad_values, grad_offset_rows = lax.map(
        row_backward, (queries, key_rows, value_rows, offset_bias, segments, log_totals, grad_mixed)
    )
    grad_bucket_rows = jnp.einsum("rhk,bk->rbh", grad_offset_rows, bucket_hot, precision=highest)
    grad_table = jnp.einsum("rg,rbh->gbh", task_onehot, grad_bucket_rows, precision=highest)
    grad_projected = jnp.concatenate(
        (
            grad_queries.reshape(total, width),
            grad_keys.reshape(total, width),
            grad_values.reshape(total, width),
        ),
        axis=1,
    )
    grad_joined = jnp.einsum(
        "nd,ne->de", normed, grad_projected, preferred_element_type=jnp.float32
    )
    grad_normed = jnp.einsum(
        "ne,de->nd", grad_projected, joined_w, preferred_element_type=jnp.float32
    )
    grad_flat_part, grad_gain_attn = norm_pull(grad_normed)
    grad_tokens = (grad_middle + grad_flat_part).reshape(row_count, length, width)
    cols_up, cols_down = (
        lax.psum_scatter(
            grad_up_full.astype(jnp.bfloat16), "an", scatter_dimension=1, tiled=True
        ).astype(jnp.float32),
        lax.psum_scatter(
            grad_down_full.astype(jnp.bfloat16), "an", scatter_dimension=0, tiled=True
        ).astype(jnp.float32),
    )
    grad_up, grad_down = (
        lax.psum_scatter(
            cols_up.astype(jnp.bfloat16), "ma", scatter_dimension=0, tiled=True
        ).astype(jnp.float32),
        lax.psum_scatter(
            cols_down.astype(jnp.bfloat16), "ma", scatter_dimension=1, tiled=True
        ).astype(jnp.float32),
    )
    grad_query, grad_key, grad_value, grad_w_out, grad_table, grad_gain_attn, grad_gain_ffn = (
        lax.psum(
            (
                grad_joined[:, :width],
                grad_joined[:, width : 2 * width],
                grad_joined[:, 2 * width :],
                grad_w_out,
                grad_table,
                grad_gain_attn,
                grad_gain_ffn,
            ),
            ("ma", "an"),
        )
    )
    return (
        output,
        grad_tokens,
        grad_query,
        grad_key,
        grad_value,
        grad_w_out,
        grad_up,
        grad_down,
        grad_table,
        grad_gain_attn,
        grad_gain_ffn,
    )


def solution(mesh):
    in_specs = (
        P(("ma", "an"), None, None),
        P(("ma", "an")),
        P(("ma", "an"), None),
        P(),
        P(),
        P(),
        P(),
        P(),
        P("ma", "an"),
        P("an", "ma"),
        P(),
        P(),
        P(),
        P(("ma", "an"), None, None),
    )
    out_specs = (
        P(("ma", "an"), None, None),
        P(("ma", "an"), None, None),
        P(),
        P(),
        P(),
        P(),
        P("ma", "an"),
        P("an", "ma"),
        P(),
        P(),
        P(),
    )
    return jax.shard_map(local, mesh=mesh, in_specs=in_specs, out_specs=out_specs, check_vma=False)
```

profile of v0, /device:TPU:0, one launch (start us, length us, event | category | flops | bytes accessed | tf_op | source)
XLA Modules:
  0.0 1382.9 jit_solution(17327542039483989079)
XLA Ops:
  61.7 358.5 %while.32 = (s32[]{:T(128)}, bf16[2,512,12,64]{1,3,2,0:T(8,128)(2,1)}, f32[2,12,512,1]{2,1,3,0:T(8,128)S(1)}, bf16[2,512,12,64]{1,3,2,0:T(8,128)(2,1)}, s32[2,51...) while((s32[]{:T(128)}, ...), condition=%wide.region_4.5_spmd, body=%wide.region_1.4_spmd.sunk | while | flops 831121408 | bytes 362676224 | solution.py:106
  108.8 39.7 %copy.111 = f32[2,8,512,1024]{3,1,2,0:T(8,128)} copy(f32[2,8,512,1024]{3,2,1,0:T(8,128)S(1)} %bitcast.228) | data formatting | bytes 67108864 | tf_op jit(solution)/shard_map/while
  148.5 22.6 %slice.82 = f32[12,523776]{1,0:T(8,128)} slice(f32[12,524288]{1,0:T(8,128)} %bitcast.231), slice={[0:12], [0:523776]} | slice | bytes 50282496 | tf_op jit(solution)/shard_map/while/body/eval_jaxpr/slice | solution.py:23
  171.1 41.2 %reshape.284 = f32[12,512,1023]{2,1,0:T(8,128)} reshape(f32[12,523776]{1,0:T(8,128)} %slice.82) | data formatting | bytes 50282496 | tf_op jit(solution)/shard_map/while/body/eval_jaxpr/reshape | solution.py:24
  212.3 13.4 slice.83
  225.6 12.6 copy.112
  272.8 39.7 %copy.111 = f32[2,8,512,1024]{3,1,2,0:T(8,128)} copy(f32[2,8,512,1024]{3,2,1,0:T(8,128)S(1)} %bitcast.228) | data formatting | bytes 67108864 | tf_op jit(solution)/shard_map/while
  312.6 22.6 %slice.82 = f32[12,523776]{1,0:T(8,128)} slice(f32[12,524288]{1,0:T(8,128)} %bitcast.231), slice={[0:12], [0:523776]} | slice | bytes 50282496 | tf_op jit(solution)/shard_map/while/body/eval_jaxpr/slice | solution.py:23
  335.2 41.2 %reshape.284 = f32[12,512,1023]{2,1,0:T(8,128)} reshape(f32[12,523776]{1,0:T(8,128)} %slice.82) | data formatting | bytes 50282496 | tf_op jit(solution)/shard_map/while/body/eval_jaxpr/reshape | solution.py:24
  376.3 13.4 slice.83
  389.7 12.6 copy.112
  448.5 15.7 %fusion.55 = bf16[1024,3072]{1,0:T(8,128)(2,1)S(1)} fusion(f32[1024,3072]{1,0:T(8,128)} %copy-done.50, bf16[1024,768]{1,0:T(8,128)(2,1)} %bitcast.245, bf16[3072,768]{1,0:T(8,128)(2,1)} %all-gather.5.cloned.1.call-done), kind=kOutput, calls=%fused_computation.71 | convolution fusion | flops 4894752768 | bytes 25165824 | tf_op jit(solution)/shard_map/nd,fd->nf/dot_general | solution.py:123
  489.9 12.3 convolution_convert_fusion.2
  506.2 615.0 %while.33 = (s32[]{:T(128)}, bf16[2,512,12,64]{1,3,2,0:T(8,128)(2,1)}, bf16[2,512,12,64]{1,3,2,0:T(8,128)(2,1)}, bf16[2,512,12,64]{1,3,2,0:T(8,128)(2,1)}, f32[2...) while((s32[]{:T(128)}, ...), condition=%wide.region_10.11_spmd, body=%wide.region_7.10_spmd.sunk | while | flops 2059515904 | bytes 669272000 | solution.py:162
  515.4 11.7 tile.27
  538.4 39.7 %copy.113 = f32[2,8,512,1024]{3,1,2,0:T(8,128)} copy(f32[2,8,512,1024]{3,2,1,0:T(8,128)S(1)} %bitcast.229) | data formatting | bytes 67108864 | tf_op jit(solution)/shard_map/while
  578.1 22.8 %slice.86 = f32[12,523776]{1,0:T(8,128)} slice(f32[12,524288]{1,0:T(8,128)} %bitcast.232), slice={[0:12], [0:523776]} | slice | bytes 50282496 | tf_op jit(solution)/shard_map/while/body/eval_jaxpr/slice | solution.py:23
  600.9 41.8 %reshape.286 = f32[12,512,1023]{2,1,0:T(8,128)} reshape(f32[12,523776]{1,0:T(8,128)} %slice.86) | data formatting | bytes 50282496 | tf_op jit(solution)/shard_map/while/body/eval_jaxpr/reshape | solution.py:24
  642.7 13.4 slice.87
  656.0 12.6 copy.114
  715.1 34.8 %reshape.287 = bf16[12,523776]{1,0:T(8,128)(2,1)} reshape(bf16[12,512,1023]{2,1,0:T(8,128)(2,1)} %pad.27.clone.2) | data formatting | bytes 25141248 | tf_op jit(solution)/shard_map/while/body/eval_jaxpr/reshape | solution.py:30
  758.4 35.9 %copy.116 = f32[2,8,512,1024]{3,2,1,0:T(8,128)} copy(f32[2,8,512,1024]{3,1,2,0:T(8,128)S(1)} %bitcast.230) | data formatting | bytes 67108864 | tf_op jit(solution)/shard_map/while
  836.0 39.7 %copy.113 = f32[2,8,512,1024]{3,1,2,0:T(8,128)} copy(f32[2,8,512,1024]{3,2,1,0:T(8,128)S(1)} %bitcast.229) | data formatting | bytes 67108864 | tf_op jit(solution)/shard_map/while
  875.8 22.6 %slice.86 = f32[12,523776]{1,0:T(8,128)} slice(f32[12,524288]{1,0:T(8,128)} %bitcast.232), slice={[0:12], [0:523776]} | slice | bytes 50282496 | tf_op jit(solution)/shard_map/while/body/eval_jaxpr/slice | solution.py:23
  898.3 54.0 %reshape.286 = f32[12,512,1023]{2,1,0:T(8,128)} reshape(f32[12,523776]{1,0:T(8,128)} %slice.86) | data formatting | bytes 50282496 | tf_op jit(solution)/shard_map/while/body/eval_jaxpr/reshape | solution.py:24
  952.4 13.4 slice.87
  965.7 12.6 copy.114
  1024.7 34.8 %reshape.287 = bf16[12,523776]{1,0:T(8,128)(2,1)} reshape(bf16[12,512,1023]{2,1,0:T(8,128)(2,1)} %pad.27.clone.2) | data formatting | bytes 25141248 | tf_op jit(solution)/shard_map/while/body/eval_jaxpr/reshape | solution.py:30
  1068.0 35.9 %copy.116 = f32[2,8,512,1024]{3,2,1,0:T(8,128)} copy(f32[2,8,512,1024]{3,1,2,0:T(8,128)S(1)} %bitcast.230) | data formatting | bytes 67108864 | tf_op jit(solution)/shard_map/while
  1166.2 43.1 %all-reduce.4 = (f32[8,32,12]{1,0,2:T(8,128)}, f32[768]{0:T(1024)}, f32[768]{0:T(1024)}) all-reduce(f32[8,32,12]{1,0,2:T(8,128)S(1)} %fusion.74, f32[768]{0:T(1024)S(1)} %get-tuple-element.333, f32[768]{0:T(1024)S(1)} %copy-done.46), channel_id=1, replica_groups=mesh['ma'=2,'an'=16] {'ma','an'}, use_global_device_ids=true, to_apply=%region_20.21 | all-reduce | flops 4608 | bytes 36864 | tf_op jit(solution)/shard_map/psum | solution.py:200
  1214.8 12.9 add_convert_fusion
  1231.4 134.6 %all-reduce.8.cloned.1.call-done = (f32[768,768]{1,0:T(8,128)}, f32[768,768]{1,0:T(8,128)}, f32[768,768]{1,0:T(8,128)}, f32[768,768]{1,0:T(8,128)}) async-done(((f32[768,768]{1,0:T(8,128)}, f32[768,768]{1,0:T(8,128)}, f32[768,768]{1,0:T(8,128)}, f32[768,768]{1,0:T(8,128)}), (f32[768,768]{1,0:T(8,128)}, f32[768,768]{1,0:T(8,128)}, f32[768,768]{1,0:T(8,128)}, ...) | async-done | bytes 9437200 | tf_op jit(solution)/shard_map/psum | solution.py:200
  (276 shorter events, 426.8 us)
Async XLA Ops:
  7.2 416.6 %copy-start = (bf16[768,768]{1,0:T(8,128)(2,1)S(1)}, bf16[768,768]{1,0:T(8,128)(2,1)}, u32[]{:S(2)}) copy-start(bf16[768,768]{1,0:T(8,128)(2,1)} %param.25) | copy-start | bytes 3538948
  7.2 19.3 %copy-start.8 = (bf16[2,512,768]{2,1,0:T(8,128)(2,1)S(1)}, bf16[2,512,768]{2,1,0:T(8,128)(2,1)}, u32[]{:S(2)}) copy-start(bf16[2,512,768]{2,1,0:T(8,128)(2,1)} %param.18) | copy-start | bytes 4718596
  7.2 19.2 %copy-start.41 = (f32[768]{0:T(1024)S(1)}, f32[768]{0:T(1024)}, u32[]{:S(2)}) copy-start(f32[768]{0:T(1024)} %param.29) | copy-start | bytes 9220
  7.2 419.8 %all-gather.3.cloned.1.call-start = ((), (), s32[]{:S(2)}) async-start(), calls=%async_computation.4 | async-start | bytes 5013504 | tf_op jit(solution)/shard_map/all_gather | solution.py:65
  16.8 431.7 %all-gather.5.cloned.1.call-start = ((), (), s32[]{:S(2)}) async-start(), calls=%async_computation.5 | async-start | bytes 5013504 | tf_op jit(solution)/shard_map/all_gather | solution.py:66
  23.0 1111.2 %reduce-scatter.11.cloned.1.call-start = ((), (), s32[]{:S(2)}) async-start(), calls=%async_computation.7 | async-start | bytes 5013504 | tf_op jit(solution)/shard_map/reduce_scatter | solution.py:187
  53.2 7.0 copy-start.43
  427.0 12.6 copy-start.27
  448.5 696.0 %reduce-scatter.9.cloned.1.call-start = ((), (), s32[]{:S(2)}) async-start(), calls=%async_computation.6 | async-start | bytes 5013504 | tf_op jit(solution)/shard_map/reduce_scatter | solution.py:184
  448.5 15.7 %copy-start.18 = (f32[1024,768]{1,0:T(8,128)S(1)}, f32[1024,768]{1,0:T(8,128)}, u32[]{:S(2)}) copy-start(f32[1024,768]{1,0:T(8,128)} %get-tuple-element.395) | copy-start | bytes 9437188
  464.3 10.9 copy-start.51
  464.3 10.9 copy-start.28
  502.2 725.6 %reduce-scatter.15.cloned.1.call-start = ((), (), s32[]{:S(2)}) async-start(), calls=%async_computation.9 | async-start | bytes 589824
  506.6 8.7 copy-start.3
  506.6 8.7 copy-start.16
  506.6 8.7 copy-start.31
  680.1 6.9 copy-start.7
  794.3 9.5 copy-start.34
  794.3 10.2 copy-start.4
  794.3 10.2 copy-start.17
  794.3 10.2 copy-start.32
  804.8 8.7 copy-start.3
  804.9 8.7 copy-start.16
  804.9 8.7 copy-start.31
  1103.9 9.5 copy-start.34
  1103.9 10.2 copy-start.4
  1103.9 10.2 copy-start.17
  1103.9 10.2 copy-start.32
  1136.1 92.8 %reduce-scatter.13.cloned.1.call-start = ((), (), s32[]{:S(2)}) async-start(), calls=%async_computation.8 | async-start | bytes 589824
  1146.4 219.6 %all-reduce.8.cloned.1.call-start = ((), (), s32[]{:S(2)}) async-start(), calls=%async_computation.10 | async-start | bytes 18874368 | tf_op jit(solution)/shard_map/psum | solution.py:200
  1156.6 9.6 copy-start.46
  1156.6 52.7 %copy-start.40 = (f32[1,4,2,128]{3,1,2,0:T(4,128)S(1)}, f32[1,4,2,128]{3,1,2,0:T(4,128)}, u32[]{:S(2)}) copy-start(f32[1,4,2,128]{3,1,2,0:T(4,128)} %copy-done.39) | copy-start | bytes 12292
  (41 other events, 141.9 us)
Sparse Core Ops, SparseCore 0:
  16.9 53.5 all-gather.2
  72.8 51.7 all-gather.4
  448.6 77.0 reduce-scatter.10
  529.9 74.6 reduce-scatter.8
  1136.2 14.5 reduce-scatter.14
  1153.0 13.1 reduce-scatter.12
  1173.0 192.9 all-reduce.7
where the time goes:
time: 1390 us; the launch traced here: 1380 us
  local copies, waits for them, and re-layouts  894 us (64%)
  matrix products  177 us (13%)
  waiting for transfers between devices  135 us (10%)
  other arithmetic  64.5 us (5%)
  blocking collectives  58.7 us (4%)
  loops' own time  38 us (3%)
  between operations  14.9 us (1%)
    while x72, local copies, waits for them, and re-layouts  344 us
    reshape x4, local copies, waits for them, and re-layouts, spread_offsets(): return tiled.reshape(heads, length, 2 * length - 1)[:, :, length - 1:]  178 us
    psum x1, waiting for transfers between devices, local(): lax.psum((grad_joined[:, :width], grad_joined[:, width:2 * width], grad_j...  135 us
    slice x4, local copies, waits for them, and re-layouts, spread_offsets(): tiled = jnp.tile(padded, (1, length))[:, :length * (2 * length - 1)]  90.5 us
    reshape x2, local copies, waits for them, and re-layouts, diagonal_sums(): wide.reshape(heads, length * (2 * length - 1))  69.6 us
    slice x4, local copies, waits for them, and re-layouts, spread_offsets(): return tiled.reshape(heads, length, 2 * length - 1)[:, :, length - 1:]  53.5 us
    another operation x4, local copies, waits for them, and re-layouts, spread_offsets(): tiled = jnp.tile(padded, (1, length))[:, :length * (2 * length - 1)]  46.3 us
    psum x1, blocking collectives, local(): lax.psum((grad_joined[:, :width], grad_joined[:, width:2 * width], grad_j...  43.1 us
  transfers between devices with their start and end apart: 7, of which 1 were waited for; matrix products, arithmetic and copies ran while one was open for 81% of the time, Pallas kernels for 0%

commit v1 on v0

v1 whole, which is shorter than its diff:
```python
import jax
import jax.numpy as jnp
from jax import lax
from jax.sharding import PartitionSpec as P
from jax.experimental import pallas as pl
from jax.experimental.pallas import tpu as pltpu

epsilon = 1e-06
highest = lax.Precision.HIGHEST


def rms_scale(values, gain_vec):
    return (
        values * lax.rsqrt(jnp.mean(values * values, axis=-1, keepdims=True) + epsilon) * gain_vec
    )


def smooth_gate(values):
    return jax.nn.gelu(values, approximate=True)


BF=jnp.bfloat16
BLK=128
NT=(((1,),(1,)),((),()))
NN=(((1,),(0,)),((),()))

def fwd_body(q_ref,k_ref,v_ref,kseg_ref,qseg_ref,f_ref,u_ref,s_ref,o_ref):
    length=q_ref.shape[0]
    nb=length//BLK
    lane=lax.broadcasted_iota(jnp.int32,(length,BLK),1)
    q=q_ref[...]*BF(0.125)
    qaug=jnp.concatenate([q,qseg_ref[...]],axis=1)
    vt=v_ref[...].astype(jnp.float32).T.astype(BF)
    k=k_ref[...]
    outs=[]
    for h in range(2):
        kaug=jnp.concatenate([jnp.where((lane>=64)==(h==1),k,BF(0)),kseg_ref[...]],axis=1)
        toep=pltpu.roll(jnp.broadcast_to(f_ref[0,h:h+1,:],(BLK,6*BLK)),0,1,stride=1,stride_axis=0)
        vaug=jnp.concatenate([vt[64*h:64*h+64],jnp.ones((16,length),BF)],axis=0)
        parts=[]
        for s in range(nb//2):
            st=lax.dot_general(kaug,qaug[256*s:256*s+256],NT,preferred_element_type=jnp.float32)
            for half in range(2):
                qb=2*s+half
                blocks={}
                m=None
                for kb in range(nb):
                    o=kb-qb
                    if abs(o)>2: continue
                    b=st[BLK*kb:BLK*kb+BLK,BLK*half:BLK*half+BLK]+toep[:,384-BLK*o:512-BLK*o]
                    blocks[kb]=b
                    m=b if m is None else jnp.maximum(m,b)
                m=jnp.max(m,axis=0,keepdims=True)
                for kb in range(nb):
                    if kb in blocks:
                        u=jnp.exp(blocks[kb]-m).astype(BF)
                    else:
                        u=jnp.zeros((BLK,BLK),BF)
                    u_ref[0,h,BLK*kb:BLK*kb+BLK,BLK*qb:BLK*qb+BLK]=u
            ot=lax.dot_general(vaug,u_ref[0,h,:,256*s:256*s+256],NN,preferred_element_type=jnp.float32)
            r=1.0/ot[64:65]
            s_ref[0,h:h+1,256*s:256*s+256]=r
            parts.append(ot[:64]*r)
        outs.append(jnp.concatenate(parts,axis=1))
    o_ref[...]=jnp.concatenate(outs,axis=0).T.astype(BF)

def fwd(proj,kseg,qseg,f,rows,length,heads):
    pairs=heads//2
    n=rows*length
    def at(off): return pl.BlockSpec((length,BLK),lambda r,p,off=off:(r,p+off))
    return pl.pallas_call(fwd_body,grid=(rows,pairs),
        in_specs=[at(0),at(pairs),at(2*pairs),
                  pl.BlockSpec((length,BLK),lambda r,p:(r,0)),pl.BlockSpec((length,BLK),lambda r,p:(r,0)),
                  pl.BlockSpec((1,2,6*BLK),lambda r,p:(r*pairs+p,0,0))],
        out_specs=[pl.BlockSpec((1,2,length,length),lambda r,p:(r*pairs+p,0,0,0)),
                   pl.BlockSpec((1,2,length),lambda r,p:(r*pairs+p,0,0)),
                   pl.BlockSpec((length,BLK),lambda r,p:(r,p))],
        out_shape=[jax.ShapeDtypeStruct((rows*pairs,2,length,length),BF),
                   jax.ShapeDtypeStruct((rows*pairs,2,length),jnp.float32),
                   jax.ShapeDtypeStruct((n,heads*64),BF)],
        compiler_params=pltpu.CompilerParams(vmem_limit_bytes=48*1024*1024),
        name="attend")(proj,proj,proj,kseg,qseg,f)

def bwd_body(q_ref,k_ref,v_ref,u_ref,s_ref,o_ref,g_ref,dq_ref,dk_ref,dv_ref,df_ref,ds_ref):
    length=q_ref.shape[0]
    nb=length//BLK
    lane=lax.broadcasted_iota(jnp.int32,(length,BLK),1)
    q=q_ref[...]*BF(0.125)
    k=k_ref[...]; v=v_ref[...]
    kt=k.astype(jnp.float32).T.astype(BF)
    inv=jnp.concatenate([jnp.broadcast_to(s_ref[0,h:h+1,:],(64,length)) for h in range(2)],axis=0).T
    g=(g_ref[...].astype(jnp.float32)*inv)
    prod=g*o_ref[...].astype(jnp.float32)
    gl=g.astype(BF)
    phi=prod.astype(BF); plo=(prod-phi.astype(jnp.float32)).astype(BF)
    rr=lax.broadcasted_iota(jnp.int32,(2*BLK,BLK),0)
    cc=lax.broadcasted_iota(jnp.int32,(2*BLK,BLK),1)
    pick=jnp.where((((rr//64)%2)==(cc//2))&(cc<4),-1.0,0.0).astype(BF)
    cen=lax.dot_general(jnp.concatenate([phi,plo],axis=1),pick,NN,preferred_element_type=jnp.float32)
    chi=cen.astype(BF); clo=(cen-chi.astype(jnp.float32)).astype(BF)
    gaug=jnp.concatenate([gl,jnp.where(lane%2==0,chi,clo)],axis=1)
    zero=BF(0)
    dqt=[]
    dv=None; dk=None
    for h in range(2):
        mine=(lane>=64)==(h==1)
        vaug=jnp.concatenate([jnp.where(mine,v,zero),jnp.where((lane//2)==h,BF(1),zero)],axis=1)
        diag=[None]*5
        for s in range(nb//2):
            dp=lax.dot_general(vaug,gaug[256*s:256*s+256],NT,preferred_element_type=jnp.float32)
            for half in range(2):
                qb=2*s+half
                for kb in range(nb):
                    o=kb-qb
                    if abs(o)>2:
                        ds_ref[h,BLK*kb:BLK*kb+BLK,BLK*qb:BLK*qb+BLK]=jnp.zeros((BLK,BLK),BF)
                        continue
                    u=u_ref[0,h,BLK*kb:BLK*kb+BLK,BLK*qb:BLK*qb+BLK].astype(jnp.float32)
                    ds=u*dp[BLK*kb:BLK*kb+BLK,BLK*half:BLK*half+BLK]
                    ds_ref[h,BLK*kb:BLK*kb+BLK,BLK*qb:BLK*qb+BLK]=ds.astype(BF)
                    diag[o+2]=ds if diag[o+2] is None else diag[o+2]+ds
        dsm=ds_ref[h]
        t=lax.dot_general(u_ref[0,h],jnp.where(mine,gl,zero),NN,preferred_element_type=jnp.float32)
        dv=t if dv is None else dv+t
        t=lax.dot_general(dsm,jnp.where(mine,q,zero),NN,preferred_element_type=jnp.float32)
        dk=t if dk is None else dk+t
        dqt.append(lax.dot_general(kt[64*h:64*h+64],dsm,NN,preferred_element_type=jnp.float32))
        wide=jnp.concatenate([jnp.zeros((BLK,BLK),jnp.float32)]+[diag[o+2] for o in (2,1,0,-1,-2)],axis=1)
        step=BLK//2
        while step:
            wide=wide[:step]+pltpu.roll(wide[step:],6*BLK-step,1)
            step//=2
        df_ref[0,h:h+1,:]=wide
    dq_ref[...]=(jnp.concatenate(dqt,axis=0).T*0.125).astype(BF)
    dk_ref[...]=dk.astype(BF)
    dv_ref[...]=dv.astype(BF)

def bwd(proj,u,inv,mixed,gmixed,rows,length,heads):
    pairs=heads//2
    n=rows*length
    def at(off): return pl.BlockSpec((length,BLK),lambda r,p,off=off:(r,p+off))
    return pl.pallas_call(bwd_body,grid=(rows,pairs),
        in_specs=[at(0),at(pairs),at(2*pairs),
                  pl.BlockSpec((1,2,length,length),lambda r,p:(r*pairs+p,0,0,0)),
                  pl.BlockSpec((1,2,length),lambda r,p:(r*pairs+p,0,0)),
                  at(0),at(0)],
        out_specs=[at(0),at(0),at(0),pl.BlockSpec((1,2,6*BLK),lambda r,p:(r*pairs+p,0,0))],
        out_shape=[jax.ShapeDtypeStruct((n,heads*64),BF)]*3+[jax.ShapeDtypeStruct((rows*pairs,2,6*BLK),jnp.float32)],
        scratch_shapes=[pltpu.VMEM((2,length,length),BF)],
        compiler_params=pltpu.CompilerParams(vmem_limit_bytes=48*1024*1024),
        name="attend_grad")(proj,proj,proj,u,inv,mixed,gmixed)

def seg_cols(segments):
    seg=segments.reshape(-1,1)
    lane=jnp.arange(BLK)[None,:]
    kseg=(lane==seg).astype(BF)
    qseg=jnp.where((lane!=seg)&(lane<4),-1e30,0.0).astype(BF)
    return kseg,qseg
def offsets_in(table_rows,buckets):
    b=buckets[128:896][::-1]
    hot=(b[None,:]==jnp.arange(table_rows.shape[1])[:,None]).astype(jnp.float32)
    f=jnp.einsum("rbh,bk->rhk",table_rows,hot,precision=lax.Precision.HIGHEST)
    rows,heads,w=f.shape
    return f.reshape(rows*heads//2,2,w),hot


def local(
    tokens,
    tasks,
    segments,
    buckets,
    w_query,
    w_key,
    w_value,
    w_out,
    w_up,
    w_down,
    bias_table,
    gain_attn,
    gain_ffn,
    cotangent,
):
    row_count = tokens.shape[0]
    length = tokens.shape[1]
    width = tokens.shape[2]
    groups = bias_table.shape[0]
    bucket_count = bias_table.shape[1]
    heads = bias_table.shape[2]
    total = row_count * length
    flat_tokens = tokens.astype(jnp.float32).reshape(total, width)
    part_up, part_down = (
        lax.all_gather(w_up, "ma", axis=0, tiled=True),
        lax.all_gather(w_down, "ma", axis=1, tiled=True),
    )
    up_full, down_full = (
        lax.all_gather(part_up, "an", axis=1, tiled=True),
        lax.all_gather(part_down, "an", axis=0, tiled=True),
    )
    normed_f, norm_pull = jax.vjp(rms_scale, flat_tokens, gain_attn)
    normed = normed_f.astype(jnp.bfloat16)
    joined_w = jnp.concatenate((w_query, w_key, w_value), axis=1)
    projected = jnp.dot(normed, joined_w, preferred_element_type=jnp.float32).astype(jnp.bfloat16)
    task_onehot = (tasks[:, None] == jnp.arange(groups, dtype=jnp.int32)[None, :]).astype(
        jnp.float32
    )
    table_rows = jnp.einsum("rg,gbh->rbh", task_onehot, bias_table, precision=highest)
    key_cols, query_cols = seg_cols(segments)
    offset_bias, bucket_hot = offsets_in(table_rows, buckets)
    weights, inverse, mixed_flat = fwd(
        projected, key_cols, query_cols, offset_bias, row_count, length, heads
    )
    middle = flat_tokens + jnp.dot(mixed_flat, w_out, preferred_element_type=jnp.float32)
    second_f, second_pull = jax.vjp(rms_scale, middle, gain_ffn)
    second = second_f.astype(jnp.bfloat16)
    up_proj = jnp.dot(second, up_full, preferred_element_type=jnp.float32)
    hidden_f, gate_pull = jax.vjp(smooth_gate, up_proj)
    hidden = hidden_f.astype(jnp.bfloat16)
    ffn_out = jnp.dot(hidden, down_full, preferred_element_type=jnp.float32)
    output = (middle + ffn_out).astype(jnp.bfloat16).reshape(row_count, length, width)
    upstream = cotangent.astype(jnp.float32).reshape(total, width)
    upstream_low = cotangent.reshape(total, width)
    grad_down_full = jnp.einsum(
        "nf,nd->fd", hidden, upstream_low, preferred_element_type=jnp.float32
    )
    grad_hidden = jnp.einsum(
        "nd,fd->nf", upstream_low, down_full, preferred_element_type=jnp.float32
    )
    grad_up_pre = gate_pull(grad_hidden)[0].astype(jnp.bfloat16)
    grad_up_full = jnp.einsum("nd,nf->df", second, grad_up_pre, preferred_element_type=jnp.float32)
    grad_second = jnp.einsum("nf,df->nd", grad_up_pre, up_full, preferred_element_type=jnp.float32)
    grad_mid_part, grad_gain_ffn = second_pull(grad_second)
    grad_middle = upstream + grad_mid_part
    grad_attn_low = grad_middle.astype(jnp.bfloat16)
    grad_w_out = jnp.einsum(
        "nd,ne->de", mixed_flat, grad_attn_low, preferred_element_type=jnp.float32
    )
    grad_mixed = jnp.einsum("ne,de->nd", grad_attn_low, w_out, preferred_element_type=jnp.float32)
    grad_mixed = grad_mixed.astype(jnp.bfloat16)
    grad_queries, grad_keys, grad_values, grad_offset_rows = bwd(
        projected, weights, inverse, mixed_flat, grad_mixed, row_count, length, heads
    )
    grad_bucket_rows = jnp.einsum(
        "rhk,bk->rbh",
        grad_offset_rows.reshape(row_count, heads, -1),
        bucket_hot,
        precision=highest,
    )
    grad_table = jnp.einsum("rg,rbh->gbh", task_onehot, grad_bucket_rows, precision=highest)
    grad_projected = jnp.concatenate((grad_queries, grad_keys, grad_values), axis=1)
    grad_joined = jnp.einsum(
        "nd,ne->de", normed, grad_projected, preferred_element_type=jnp.float32
    )
    grad_normed = jnp.einsum(
        "ne,de->nd", grad_projected, joined_w, preferred_element_type=jnp.float32
    )
    grad_flat_part, grad_gain_attn = norm_pull(grad_normed)
    grad_tokens = (grad_middle + grad_flat_part).reshape(row_count, length, width)
    cols_up, cols_down = (
        lax.psum_scatter(
            grad_up_full.astype(jnp.bfloat16), "an", scatter_dimension=1, tiled=True
        ).astype(jnp.float32),
        lax.psum_scatter(
            grad_down_full.astype(jnp.bfloat16), "an", scatter_dimension=0, tiled=True
        ).astype(jnp.float32),
    )
    grad_up, grad_down = (
        lax.psum_scatter(
            cols_up.astype(jnp.bfloat16), "ma", scatter_dimension=0, tiled=True
        ).astype(jnp.float32),
        lax.psum_scatter(
            cols_down.astype(jnp.bfloat16), "ma", scatter_dimension=1, tiled=True
        ).astype(jnp.float32),
    )
    grad_query, grad_key, grad_value, grad_w_out, grad_table, grad_gain_attn, grad_gain_ffn = (
        lax.psum(
            (
                grad_joined[:, :width],
                grad_joined[:, width : 2 * width],
                grad_joined[:, 2 * width :],
                grad_w_out,
                grad_table,
                grad_gain_attn,
                grad_gain_ffn,
            ),
            ("ma", "an"),
        )
    )
    return (
        output,
        grad_tokens,
        grad_query,
        grad_key,
        grad_value,
        grad_w_out,
        grad_up,
        grad_down,
        grad_table,
        grad_gain_attn,
        grad_gain_ffn,
    )


def solution(mesh):
    in_specs = (
        P(("ma", "an"), None, None),
        P(("ma", "an")),
        P(("ma", "an"), None),
        P(),
        P(),
        P(),
        P(),
        P(),
        P("ma", "an"),
        P("an", "ma"),
        P(),
        P(),
        P(),
        P(("ma", "an"), None, None),
    )
    out_specs = (
        P(("ma", "an"), None, None),
        P(("ma", "an"), None, None),
        P(),
        P(),
        P(),
        P(),
        P("ma", "an"),
        P("an", "ma"),
        P(),
        P(),
        P(),
    )
    return jax.shard_map(local, mesh=mesh, in_specs=in_specs, out_specs=out_specs, check_vma=False)
```

time: 1390 us -> 537 us (0.39)
  local copies, waits for them, and re-layouts: 894 us -> 39 us
  waiting for transfers between devices: 135 us -> 262 us
  matrix products: 177 us -> 96.7 us
  other arithmetic: 64.5 us -> 10.6 us
  Pallas kernels: 0 us -> 46.7 us
  loops' own time: 38 us -> 0 us
    while x80 -> x0, local copies, waits for them, and re-layouts: 366 us -> none
    reshape x10 -> x2, local copies, waits for them, and re-layouts: 263 us -> 0.09 us  [the longest x1 0.05 us: local(): grad_offset_rows.reshape(row_count, heads, -1)]
    slice x12 -> x1, local copies, waits for them, and re-layouts: 153 us -> 0.69 us  [offsets_in(): b = buckets[128:896][::-1]]
    dot_general x16 -> x2, matrix products: 74.8 us -> 0.36 us  [the longest x1 0.18 us: offsets_in(): jnp.einsum('rbh,bk->rhk', table_rows, hot, precision=lax.Precision.HIGHEST)]
    reduce_scatter x1, waiting for transfers between devices: 0.01 us -> 67 us  [local(): lax.psum_scatter(grad_up_full.astype(jnp.bfloat16), 'an', scatter_dimensi...]
    another operation x8 -> x0, local copies, waits for them, and re-layouts: 51.6 us -> none  [the longest x4 46.3 us: spread_offsets(): tiled = jnp.tile(padded, (1, length))[:, :length * (2 * length - 1)]]
    pallas_call x0 -> x2, Pallas kernels: none -> 46.7 us  [the longest x1 23.6 us: bwd(): pl.pallas_call(bwd_body, grid=(rows, pairs), in_specs=[at(0), at(pairs),...]
    another operation x2 -> x0, loops' own time: 38 us -> none  [the longest x1 29.8 us: local(): lax.map(row_forward, (queries, key_rows, value_rows, offset_bias, segments))]
  transfers between devices with their start and end apart: 7 -> 7, of which waited for: 1 -> 5; matrix products, arithmetic and copies ran while one was open for 81% -> 24% of each run, Pallas kernels for 0% -> 9%
where the time goes in v1:
time: 537 us; the launch traced here: 528 us
  waiting for transfers between devices  262 us (49%)
  matrix products  96.7 us (18%)
  blocking collectives  57.3 us (11%)
  Pallas kernels  46.7 us (9%)
  local copies, waits for them, and re-layouts  39 us (7%)
  between operations  14.9 us (3%)
  other arithmetic  10.6 us (2%)
    psum x1, waiting for transfers between devices, local(): lax.psum((grad_joined[:, :width], grad_joined[:, width:2 * width], grad_j...  142 us
    reduce_scatter x1, waiting for transfers between devices, local(): lax.psum_scatter(grad_up_full.astype(jnp.bfloat16), 'an', scatter_dimensi...  67 us
    psum x1, blocking collectives, local(): lax.psum((grad_joined[:, :width], grad_joined[:, width:2 * width], grad_j...  41.7 us
    all_gather x1, waiting for transfers between devices, local(): lax.all_gather(part_down, 'an', axis=0, tiled=True)  32.5 us
    unnamed x60, local copies, waits for them, and re-layouts  30.6 us
    pallas_call x1, Pallas kernels, bwd(): pl.pallas_call(bwd_body, grid=(rows, pairs), in_specs=[at(0), at(pairs),...  23.6 us
    pallas_call x1, Pallas kernels, fwd(): pl.pallas_call(fwd_body, grid=(rows, pairs), in_specs=[at(0), at(pairs),...  23.2 us
    dot_general x1, matrix products, local(): jnp.einsum('nd,fd->nf', upstream_low, down_full, preferred_element_type=j...  14.1 us
  transfers between devices with their start and end apart: 7, of which 5 were waited for; matrix products, arithmetic and copies ran while one was open for 24% of the time, Pallas kernels for 9%

profile of v1, /device:TPU:0, one launch (start us, length us, event | category | flops | bytes accessed | tf_op | source)
XLA Modules:
  0.0 527.7 jit_solution(10003542376636793431)
XLA Ops:
  7.2 9.5 %all_gather.12 = bf16[768,192]{0,1:T(8,128)(2,1)} all-gather(bf16[384,192]{0,1:T(8,128)(2,1)} %param.22), channel_id=1, replica_groups=mesh['ma'=2,'an'=16] {'ma'}, dimensions={0}, use_global_device_ids=true | all-gather | bytes 442368 | tf_op jit(solution)/shard_map/all_gather | solution.py:192
  16.8 6.1 %all_gather.14 = bf16[192,768]{1,0:T(8,128)(2,1)} all-gather(bf16[192,384]{1,0:T(8,128)(2,1)} %param.23), channel_id=1, replica_groups=mesh['ma'=2,'an'=16] {'ma'}, dimensions={1}, use_global_device_ids=true | all-gather | bytes 442368 | tf_op jit(solution)/shard_map/all_gather | solution.py:193
  24.5 1.8 fusion.13
  32.0 5.4 %convolution_convert_fusion.q_ref.k_ref.v_ref = bf16[1024,2304]{1,0:T(8,128)(2,1)} fusion(bf16[1024,768]{1,0:T(8,128)(2,1)S(1)} %fusion.11, bf16[768,2304]{1,0:T(8,128)(2,1)S(1)} %constant_dynamic-update-slice_fusion), kind=kOutput, calls=%fused_computation.10 | convolution fusion | flops 3626237952 | bytes 9830400 | tf_op jit(solution)/shard_map/dot_general | solution.py:202
  37.5 23.2 %attend.1 = (bf16[12,2,512,512]{3,2,1,0:T(8,128)(2,1)}, f32[12,2,512]{2,1,0:T(2,128)S(1)}, bf16[1024,768]{1,0:T(8,128)(2,1)S(1)}) custom-call(bf16[1024,2304]{1,0:T(8,128)(2,1)} %convolution_convert_fusion.q_ref.k_ref.v_ref, bf16[1024,2304]{1,0:T(8,128)(2,1)} %convolution_convert_fusion.q_ref.k_ref.v_ref, ...), custom_call_target="tpu_custom_call" | custom-call | tf_op jit(solution)/shard_map/attend/pallas_call | solution.py:71
  60.6 3.1 multiply_reduce_fusion.2
  63.7 6.9 %all-gather.3.cloned.1.call-done = bf16[768,3072]{0,1:T(8,128)(2,1)} async-done(((bf16[768,192]{0,1:T(8,128)(2,1)}), bf16[768,3072]{0,1:T(8,128)(2,1)}) %all-gather.3.cloned.1.call-update) | async-done | bytes 4718608 | tf_op jit(solution)/shard_map/all_gather | solution.py:196
  70.6 8.1 %fusion.35 = f32[1024,3072]{1,0:T(8,128)S(1)} fusion(bf16[768,3072]{0,1:T(8,128)(2,1)} %all-gather.3.cloned.1.call-done, f32[1024,768]{1,0:T(8,128)} %get-tuple-element.40, f32[768]{0:T(1024)S(1)} %copy-done.19, f32[1024]{0:T(1024)S(1)} %fusion.29), kind=kOutput, calls=%fused_computation.69 | convolution fusion | flops 4834197504 | bytes 20454400 | tf_op jit(solution)/shard_map/dot_general | solution.py:215
  78.7 4.5 copy-done.21
  83.2 8.8 %convolution_convert_fusion.1 = bf16[3072,768]{1,0:T(8,128)(2,1)} fusion(bf16[1024,768]{1,0:T(8,128)(2,1)S(1)} %bitcast.62, f32[1024,3072]{1,0:T(8,128)S(1)} %fusion.35), kind=kOutput, calls=%fused_computation.11 | convolution fusion | flops 4862509056 | bytes 18874368 | tf_op jit(solution)/shard_map/nf,nd->fd/dot_general | solution.py:222
  92.2 32.5 %all-gather.5.cloned.1.call-done = bf16[3072,768]{1,0:T(8,128)(2,1)} async-done(((bf16[192,768]{1,0:T(8,128)(2,1)}), bf16[3072,768]{1,0:T(8,128)(2,1)}) %all-gather.5.cloned.1.call-update) | async-done | bytes 4718608 | tf_op jit(solution)/shard_map/all_gather | solution.py:197
  124.7 14.1 %fusion.6 = bf16[1024,3072]{1,0:T(8,128)(2,1)S(1)} fusion(f32[1024,3072]{1,0:T(8,128)} %copy-done.21, bf16[1024,768]{1,0:T(8,128)(2,1)S(1)} %bitcast.63, bf16[3072,768]{1,0:T(8,128)(2,1)} %all-gather.5.cloned.1.call-done), kind=kOutput, calls=%fused_computation.8 | convolution fusion | flops 4894752768 | bytes 25165824 | tf_op jit(solution)/shard_map/nd,fd->nf/dot_general | solution.py:225
  138.8 2.7 copy-done.22
  141.5 7.3 %convolution_convert_fusion.2 = bf16[768,3072]{0,1:T(8,128)(2,1)} fusion(bf16[1024,3072]{1,0:T(8,128)(2,1)S(1)} %fusion.6, f32[1024,768]{1,0:T(8,128)S(1)} %copy-done.6, f32[768]{0:T(1024)S(1)} %copy-done.19, f32[1024]{0:T(1024)S(1)} %fusion.29), kind=kOutput, calls=%fused_computation.12 | convolution fusion | flops 4836556800 | bytes 14162944 | tf_op jit(solution)/shard_map/nd,nf->df/dot_general | solution.py:229
  148.9 9.5 %multiply_reduce_fusion = (f32[768]{0:T(1024)S(1)}, f32[1024]{0:T(1024)S(1)}, f32[1024,768]{1,0:T(8,128)S(1)}) fusion(f32[1024,768]{1,0:T(8,128)} %get-tuple-element.40, f32[1024]{0:T(1024)S(1)} %fusion.29, f32[768]{0:T(1024)S(1)} %copy-done.19, bf16[1024,3072]{1,0:T(8,128)(2,1)} %copy-done.22, bf16[768,3072]{0,1:T(8,128)(2,1)} %all-gather.3.cloned.1.call-done), kind=kOutput, calls=%fused_computation.28 | convolution fusion | flops 4836554752 | bytes 17315840 | tf_op jit(solution)/shard_map/nf,df->nd/dot_general | solution.py:230
  159.3 2.6 convolution_convert_fusion.3.g_ref
  161.9 23.6 %attend_grad.1 = (bf16[1024,768]{1,0:T(8,128)(2,1)S(1)}, bf16[1024,768]{1,0:T(8,128)(2,1)S(1)}, bf16[1024,768]{1,0:T(8,128)(2,1)S(1)}, f32[12,2,768]{2,1,0:T(2,128)S(1)}) custom-call(bf16[1024,2304]{1,0:T(8,128)(2,1)} %convolution_convert_fusion.q_ref.k_ref.v_ref, bf16[1024,2304]{1,0:T(8,128)(2,1)} %convolution_convert_fusion.q_ref.k_ref.v_ref, ...), custom_call_target="tpu_custom_call" | custom-call | tf_op jit(solution)/shard_map/attend_grad/pallas_call | solution.py:142
  189.4 13.3 %reduce-scatter.11.cloned.1.call-done = bf16[192,768]{1,0:T(8,128)(2,1)} async-done(((bf16[3072,768]{1,0:T(8,128)(2,1)}), bf16[192,768]{1,0:T(8,128)(2,1)}) %reduce-scatter.11.cloned.1.call-update) | async-done | bytes 294928 | tf_op jit(solution)/shard_map/reduce_scatter | solution.py:262
  202.7 1.9 copy.29
  204.9 9.7 %fusion.37 = f32[768,2304]{1,0:T(8,128)} fusion(bf16[1024,768]{1,0:T(8,128)(2,1)} %copy-done.12, bf16[1024,2304]{1,0:T(8,128)(2,1)} %constant_dynamic-update-slice_fusion.3), kind=kOutput, calls=%fused_computation.71 | convolution fusion | flops 3623878656 | bytes 13369344 | tf_op jit(solution)/shard_map/nd,ne->de/dot_general | solution.py:250
  214.5 67.0 %reduce-scatter.9.cloned.1.call-done = bf16[768,192]{0,1:T(8,128)(2,1)} async-done(((bf16[768,3072]{0,1:T(8,128)(2,1)}), bf16[768,192]{0,1:T(8,128)(2,1)}) %reduce-scatter.9.cloned.1.call-update) | async-done | bytes 294928 | tf_op jit(solution)/shard_map/reduce_scatter | solution.py:259
  281.5 1.9 copy.27
  283.4 4.8 fusion.15
  288.3 6.2 %fusion.36 = (f32[768,768]{1,0:T(8,128)}, f32[768,768]{1,0:T(8,128)}, f32[768,768]{1,0:T(8,128)}) fusion(f32[768,2304]{1,0:T(8,128)} %fusion.37), kind=kLoop, calls=%fused_computation.70 | loop fusion | bytes 14155776 | tf_op jit(solution)/shard_map/slice | solution.py:279
  295.9 9.1 %fusion.12 = (f32[768]{0:T(1024)S(1)}, f32[1024]{0:T(1024)S(1)}, f32[1024,768]{1,0:T(8,128)}) fusion(bf16[2,512,768]{2,1,0:T(8,128)(2,1)S(1)} %copy-done.4, f32[1024]{0:T(1024)S(1)} %rsqrt.20, f32[768]{0:T(1024)S(1)} %copy-done.18, bf16[1024,2304]{1,0:T(8,128)(2,1)} %constant_dynamic-update-slice_fusion.3, bf16[768,2304]{1,0:T(8,128)(2,1)} %copy-done.17), kind=kOutput, calls=%fused_computation.25 | convolution fusion | flops 3629381888 | bytes 12990464 | tf_op jit(solution)/shard_map/ne,de->nd/dot_general | solution.py:253
  305.1 41.7 %all-reduce = (f32[8,32,12]{1,0,2:T(8,128)}, f32[768]{0:T(1024)}, f32[768]{0:T(1024)}) all-reduce(f32[8,32,12]{1,0,2:T(8,128)S(1)} %fusion.27, f32[768]{0:T(1024)S(1)} %get-tuple-element.27, f32[768]{0:T(1024)S(1)} %get-tuple-element.25), channel_id=1, replica_groups=mesh['ma'=2,'an'=16] {'ma','an'}, use_global_device_ids=true, to_apply=%region_12.13 | all-reduce | flops 4608 | bytes 36864 | tf_op jit(solution)/shard_map/psum | solution.py:275
  346.8 5.5 %fusion.8 = f32[1024,768]{1,0:T(8,128)} fusion(f32[1024,768]{1,0:T(8,128)} %copy-done.5, bf16[2,512,768]{2,1,0:T(8,128)(2,1)S(1)} %copy-done.4, f32[1024,768]{1,0:T(8,128)} %get-tuple-element.42, f32[1024]{0:T(1024)S(1)} %multiply_multiply_fusion.2, f32[768]{0:T(1024)S(1)} %copy-done.18, f32[1024]{0:T(1024)S(1)} %rsqrt.20), kind=kLoop, calls=%fused_computation.16 | loop fusion | flops 5505024 | bytes 11021312 | tf_op jit(solution)/shard_map/add | solution.py:257
  352.4 12.7 %add_convert_fusion = bf16[1024,768]{1,0:T(8,128)(2,1)} fusion(f32[1024,768]{1,0:T(8,128)S(1)} %copy-done.8, bf16[3072,768]{1,0:T(8,128)(2,1)} %all-gather.5.cloned.1.call-done, f32[1024,3072]{1,0:T(8,128)} %copy-done.21), kind=kOutput, calls=%fused_computation.30 | convolution fusion | flops 4861722624 | bytes 22020096 | tf_op jit(solution)/shard_map/dot_general | solution.py:218
  368.7 141.9 %all-reduce.4.cloned.1.call-done = (f32[768,768]{1,0:T(8,128)}, f32[768,768]{1,0:T(8,128)}, f32[768,768]{1,0:T(8,128)}, f32[768,768]{1,0:T(8,128)}) async-done(((f32[768,768]{1,0:T(8,128)}, f32[768,768]{1,0:T(8,128)}, f32[768,768]{1,0:T(8,128)}, f32[768,768]{1,0:T(8,128)}), (f32[768,768]{1,0:T(8,128)}, f32[768,768]{1,0:T(8,128)}, f32[768,768]{1,0:T(8,128)}, ...) | async-done | bytes 9437200 | tf_op jit(solution)/shard_map/psum | solution.py:275
  510.6 3.4 copy.45
  514.0 1.4 copy.46
  519.0 1.4 copy.48
  (91 shorter events, 21.4 us)
Async XLA Ops:
  7.2 53.5 %copy-start = (bf16[768,768]{1,0:T(8,128)(2,1)S(1)}, bf16[768,768]{1,0:T(8,128)(2,1)}, u32[]{:S(2)}) copy-start(bf16[768,768]{1,0:T(8,128)(2,1)} %param.21) | copy-start | bytes 3538948
  7.2 20.5 %copy-start.14 = (bf16[768,768]{1,0:T(8,128)(2,1)S(1)}, bf16[768,768]{1,0:T(8,128)(2,1)}, u32[]{:S(2)}) copy-start(bf16[768,768]{1,0:T(8,128)(2,1)} %param.18) | copy-start | bytes 3538948
  7.2 63.4 %all-gather.3.cloned.1.call-start = ((), (), s32[]{:S(2)}) async-start(), calls=%async_computation.4 | async-start | bytes 5013504 | tf_op jit(solution)/shard_map/all_gather | solution.py:196
  16.8 108.0 %all-gather.5.cloned.1.call-start = ((), (), s32[]{:S(2)}) async-start(), calls=%async_computation.5 | async-start | bytes 5013504 | tf_op jit(solution)/shard_map/all_gather | solution.py:197
  23.0 179.7 %reduce-scatter.11.cloned.1.call-start = ((), (), s32[]{:S(2)}) async-start(), calls=%async_computation.7 | async-start | bytes 5013504 | tf_op jit(solution)/shard_map/reduce_scatter | solution.py:262
  27.6 1.3 copy-start.15
  27.6 1.6 copy-start.16
  28.9 1.5 copy-start.3
  28.9 1.5 copy-start.18
  29.3 8.1 %copy-start.17 = (bf16[768,2304]{1,0:T(8,128)(2,1)}, bf16[768,2304]{1,0:T(8,128)(2,1)S(1)}, u32[]{:S(2)}) copy-start(bf16[768,2304]{1,0:T(8,128)(2,1)S(1)} %constant_dynamic-update-slice_fusion) | copy-start | bytes 10616836
  30.9 1.1 copy-start.12
  60.6 3.1 copy-start.1
  60.6 10.0 %copy-start.19 = (f32[768]{0:T(1024)S(1)}, f32[768]{0:T(1024)}, u32[]{:S(2)}) copy-start(f32[768]{0:T(1024)} %param.26) | copy-start | bytes 9220
  70.6 12.6 %copy-start.13 = (bf16[2,512,768]{2,1,0:T(8,128)(2,1)S(1)}, bf16[2,512,768]{2,1,0:T(8,128)(2,1)}, u32[]{:S(2)}) copy-start(bf16[2,512,768]{2,1,0:T(8,128)(2,1)} %param.27) | copy-start | bytes 4718596
  78.7 4.5 copy-start.21
  92.0 189.5 %reduce-scatter.9.cloned.1.call-start = ((), (), s32[]{:S(2)}) async-start(), calls=%async_computation.6 | async-start | bytes 5013504 | tf_op jit(solution)/shard_map/reduce_scatter | solution.py:259
  124.7 16.8 %copy-start.6 = (f32[1024,768]{1,0:T(8,128)S(1)}, f32[1024,768]{1,0:T(8,128)}, u32[]{:S(2)}) copy-start(f32[1024,768]{1,0:T(8,128)} %get-tuple-element.40) | copy-start | bytes 9437188
  138.8 2.7 copy-start.22
  148.8 216.2 %reduce-scatter.15.cloned.1.call-start = ((), (), s32[]{:S(2)}) async-start(), calls=%async_computation.9 | async-start | bytes 589824
  148.9 9.5 %copy-start.7 = (f32[1024,768]{1,0:T(8,128)S(1)}, f32[1024,768]{1,0:T(8,128)}, u32[]{:S(2)}) copy-start(f32[1024,768]{1,0:T(8,128)} %get-tuple-element.40) | copy-start | bytes 9437188
  159.3 2.6 copy-start.5
  204.6 78.8 %copy-start.2 = (bf16[1024,768]{1,0:T(8,128)(2,1)S(1)}, bf16[1024,768]{1,0:T(8,128)(2,1)}, u32[]{:S(2)}) copy-start(bf16[1024,768]{1,0:T(8,128)(2,1)} %copy-done.1) | copy-start | bytes 4718596
  204.6 161.5 %reduce-scatter.13.cloned.1.call-start = ((), (), s32[]{:S(2)}) async-start(), calls=%async_computation.8 | async-start | bytes 589824
  283.4 227.2 %all-reduce.4.cloned.1.call-start = ((), (), s32[]{:S(2)}) async-start(), calls=%async_computation.10 | async-start | bytes 18874368 | tf_op jit(solution)/shard_map/psum | solution.py:275
  294.5 0.7 copy-start.20
  294.5 1.4 copy-start.4
  346.8 5.5 %copy-start.8 = (f32[1024,768]{1,0:T(8,128)S(1)}, f32[1024,768]{1,0:T(8,128)}, u32[]{:S(2)}) copy-start(f32[1024,768]{1,0:T(8,128)} %get-tuple-element.40) | copy-start | bytes 9437188
  510.6 3.4 copy-start.11
  514.0 2.5 copy-start.10
  516.5 2.5 copy-start.9
Sparse Core Ops, SparseCore 0:
  16.9 53.6 all-gather.2
  72.9 51.8 all-gather.4
  128.6 74.0 reduce-scatter.10
  206.9 74.5 reduce-scatter.8
  283.6 12.1 reduce-scatter.14
  298.0 13.1 reduce-scatter.12
  317.9 192.6 all-reduce.3
